TPU v7x, 512 devices: a whole 4x4x16 slice. The times are simulated.
512 devices in a mesh: req: 16 (over x, y), tp: 32 (over z, core).
Axes of the slice: x: 4, y: 4, z: 16, core: 2. Of those that a mesh axis runs over, the one named last changes fastest.
Arguments:
- tokens: bfloat16 [512, 16384], P(('req', 'tp')), may hold values from -6 to 6
- weight_codes: bfloat16 [16384, 53248], P('req', 'tp'), may hold values from -8 to 7, as said below
- weight_scales: bfloat16 [128, 53248], P('req', 'tp'), may hold values from 0.00077819824 to 0.003112793
- adapter_down: bfloat16 [64, 16384, 64], P('req', 'tp'), may hold values from -0.046875 to 0.046875
- adapter_up: bfloat16 [64, 64, 53248], P('req', None, 'tp'), may hold values from -0.375 to 0.375
- row_adapter: int32 [512], replicated, may hold values from 0 to 63, as said below
- adapter_slot: int32 [64], replicated, may hold values from 0 to 63, as said below
- live_rows: int32 [16], replicated, may hold values from 8 to 32, as said below
Outputs:
- projected: bfloat16 [512, 53248], P('req', 'tp')
Inputs may be any that keep to these rules, and one draw needn't show every extreme that they name: `row_adapter`: the rows of one group name at most one adapter homed on each req device (adapter a is homed on req device adapter_slot[a] // 4); in every draw some group names an adapter of every req device, and every adapter is named. A permutation: adapter a lies at index adapter_slot[a] of the first dimension of adapter_down and adapter_up. `live_rows`: rows of a group at positions at or past its count are padding; some group is full. `weight_codes`: Integers.
All inputs are finite; a program needn't handle non-finite values.
Results may differ from a plain program's by a relative error of at most 0.015.
Values may be sent and summed in bfloat16 or wider, within the bound.
A program may use at most 64 MiB of HBM per device.

v0:
```python
import jax
import jax.numpy as jnp
from jax import lax
from jax.sharding import PartitionSpec as P

adapter_scale = 2.0


def body(
    tokens,
    weight_codes,
    weight_scales,
    adapter_down,
    adapter_up,
    row_adapter,
    adapter_slot,
    live_rows,
):
    home_count = lax.axis_size("req")
    lane_count = lax.axis_size("tp")
    group_index = lax.axis_index("req")
    lane_index = lax.axis_index("tp")
    local_rows = tokens.shape[0]
    group_rows = local_rows * lane_count
    model_width = tokens.shape[1]
    block_width = model_width // home_count
    lane_width = model_width // lane_count
    columns = weight_codes.shape[1]
    per_home = adapter_down.shape[0]
    rank_width = adapter_down.shape[2]
    scale_count = weight_scales.shape[0]
    weight = (
        (
            weight_codes.reshape(scale_count, block_width // scale_count, columns).astype(
                jnp.float32
            )
            * weight_scales.astype(jnp.float32)[:, None, :]
        )
        .reshape(block_width, columns)
        .astype(jnp.bfloat16)
    )
    grouped = lax.all_gather(tokens, "tp", axis=0, tiled=True)
    gathered = lax.all_to_all(
        grouped.reshape(group_rows, home_count, block_width),
        "req",
        split_axis=1,
        concat_axis=1,
        tiled=True,
    )
    features = lax.dynamic_slice_in_dim(grouped, lane_index * lane_width, lane_width, 1)
    slots_all = adapter_slot[row_adapter]
    home_all = slots_all // per_home
    local_all = slots_all % per_home
    slot_range = jnp.arange(per_home, dtype=jnp.int32)
    wanted = jnp.any(
        (home_all.reshape(home_count, group_rows, 1) == group_index)
        & (local_all.reshape(home_count, group_rows, 1) == slot_range[None, None, :]),
        axis=1,
    ).astype(jnp.bfloat16)
    send_down = (
        jnp.dot(
            wanted,
            adapter_down.reshape(per_home, lane_width * rank_width),
            preferred_element_type=jnp.float32,
        )
        .astype(jnp.bfloat16)
        .reshape(home_count, lane_width, rank_width)
    )
    send_up = (
        jnp.dot(
            wanted,
            adapter_up.reshape(per_home, rank_width * columns),
            preferred_element_type=jnp.float32,
        )
        .astype(jnp.bfloat16)
        .reshape(home_count, rank_width, columns)
    )
    arrived_down, arrived_up = (
        lax.all_to_all(send_down, "req", split_axis=0, concat_axis=0, tiled=True),
        lax.all_to_all(send_up, "req", split_axis=0, concat_axis=0, tiled=True),
    )
    own_homes = lax.dynamic_slice_in_dim(home_all, group_index * group_rows, group_rows)
    selector = (own_homes[:, None] == jnp.arange(home_count, dtype=jnp.int32)[None, :]).astype(
        jnp.float32
    )
    projected_all = jnp.einsum(
        "rd,hdk->rhk", features, arrived_down, preferred_element_type=jnp.float32
    )
    partial_low = jnp.sum(projected_all * selector[:, :, None], axis=1)
    reduced = lax.psum(partial_low, "tp").astype(jnp.bfloat16)
    live_limit = lax.dynamic_index_in_dim(live_rows, group_index, keepdims=False)
    live_mask = jnp.arange(group_rows, dtype=jnp.int32) < live_limit
    summed = lax.psum_scatter(
        jnp.einsum("rgd,df->grf", gathered, weight, preferred_element_type=jnp.float32)
        .reshape(lax.axis_size("req") * group_rows, columns)
        .astype(jnp.bfloat16),
        "req",
        scatter_dimension=0,
        tiled=True,
    ).astype(jnp.float32)
    expanded = (selector.astype(jnp.bfloat16)[:, :, None] * reduced[:, None, :]).reshape(
        group_rows, home_count * rank_width
    )
    adapter_delta = jnp.dot(
        expanded,
        arrived_up.reshape(home_count * rank_width, columns),
        preferred_element_type=jnp.float32,
    )
    total = summed + adapter_scale * adapter_delta
    return jnp.where(live_mask[:, None], total, 0.0).astype(jnp.bfloat16)


def solution(mesh):
    in_specs = (
        P(("req", "tp"), None),
        P("req", "tp"),
        P("req", "tp"),
        P("req", "tp", None),
        P("req", None, "tp"),
        P(),
        P(),
        P(),
    )
    out_specs = P("req", "tp")
    return jax.shard_map(body, mesh=mesh, in_specs=in_specs, out_specs=out_specs, check_vma=False)
```

profile of v0, /device:TPU:6, one launch (start us, length us, event | category | flops | bytes accessed | tf_op | source)
XLA Modules:
  0.0 290.6 jit_solution(12213355746567521805)
XLA Ops:
  6.5 0.0 all-gather.3.cloned.1.call-start
  6.5 0.7 all-gather.3.cloned.1.call-update
  7.3 1.6 fusion.26
  8.9 2.1 fusion.25
  10.9 2.1 fusion.24
  13.0 2.1 fusion.23
  15.1 0.0 copy-start.5
  15.1 0.0 copy-start.4
  15.1 0.0 copy-start.3
  15.1 70.6 %all-gather.3.cloned.1.call-done = bf16[32,1,16384]{2,1,0:T(2,128)(2,1)} async-done(((bf16[1,1,16384]{2,1,0:T(2,128)(2,1)}), bf16[32,1,16384]{2,1,0:T(2,128)(2,1)}) %all-gather.3.cloned.1.call-update) | async-done | bytes 1048592 | tf_op jit(solution)/shard_map/all_gather | solution.py:42
  85.7 7.8 %reduce = bf16[32,16384]{1,0:T(8,128)(2,1)S(1)} reduce(bf16[32,1,16384]{2,1,0:T(2,128)(2,1)} %all-gather.3.cloned.1.call-done, bf16[]{:T(256)} %constant.127), dimensions={1}, to_apply=%all-gather.reduce_sub_computation | reduce | bytes 2097154 | tf_op jit(solution)/shard_map/all_gather | solution.py:42
  93.5 0.0 copy-start.2
  93.5 1.1 copy.28
  94.6 7.3 %all-to-all-start = ((bf16[32,16,1024]{2,0,1:T(8,128)(2,1)}), bf16[32,16,1024]{2,0,1:T(8,128)(2,1)}, u32[]{:S(2)}, u32[]{:S(2)}) async-start(bf16[32,16,1024]{2,0,1:T(8,128)(2,1)} %bitcast.106), calls=%async_computation | async-start | bytes 2097152 | tf_op jit(solution)/shard_map/all_to_all | solution.py:43
  101.8 0.0 copy-done.5
  101.9 40.2 %add_select_fusion.2 = (s32[512]{0:T(512)S(1)}, s32[512]{0:T(512)S(1)}) fusion(s32[]{:T(128)} %bitcast.69, s32[]{:T(128)} %bitcast.68, s32[]{:T(128)} %bitcast.67, s32[]{:T(128)} %bitcast.66, s32[]{:T(128)} %bitcast.65, s32[]{:T(128)} %bitcast.64, s32[]{:T(128)} %bitcast.63, s32[]{:T(128)} %bitcast.62, s32[]{:T(128)} %bitcast.61, s32[]{:T(128)} %bitcast.60, ...), kind=kLoop, calls=%fused_computation.34 | loop fusion | flops 73728 | bytes 6400 | tf_op jit(solution)/shard_map/jit(floor_divide)/jit(_where)/select_n | solution.py:52
  142.0 0.1 gather.6
  142.1 0.0 copy-done.4
  142.1 0.0 copy-done.3
  142.1 0.3 copy.19
  142.4 0.4 reshape.124
  142.8 0.0 copy-done.2
  142.8 1.6 copy.23
  144.4 0.1 fusion.15
  144.6 0.5 convolution_convert_fusion.1
  145.1 2.3 reshape.125
  147.4 1.7 copy.20
  149.1 4.4 %fusion = bf16[1024,1664]{1,0:T(8,128)(2,1)} fusion(bf16[1024,1664]{1,0:T(8,128)(2,1)} %param.9, f32[8,1664]{1,0:T(8,128)S(1)} %convert_element_type.53), kind=kLoop, calls=%fused_computation.3 | loop fusion | flops 5111808 | bytes 6868992 | tf_op jit(solution)/shard_map/convert_element_type | solution.py:40
  153.4 0.0 all-to-all-done
  153.4 7.2 %all-to-all-start.1 = ((bf16[16,512,64]{1,2,0:T(8,128)(2,1)}), bf16[16,512,64]{1,2,0:T(8,128)(2,1)S(1)}, u32[]{:S(2)}, u32[]{:S(2)}) async-start(bf16[16,512,64]{1,2,0:T(8,128)(2,1)} %copy.20), calls=%async_computation.2 | async-start | bytes 2097152 | tf_op jit(solution)/shard_map/all_to_all | solution.py:79
  160.7 0.2 reduce-scatter.2.cloned.1.call-start
  160.9 5.6 %fusion.3 = bf16[1664,32,16]{0,1,2:T(8,128)(2,1)} fusion(bf16[32,16,1024]{2,0,1:T(8,128)(2,1)} %all-to-all-done, bf16[1024,1664]{1,0:T(8,128)(2,1)} %fusion), kind=kOutput, calls=%fused_computation.6 | convolution fusion | flops 1745682432 | bytes 6160384 | tf_op jit(solution)/shard_map/rgd,df->grf/dot_general | solution.py:94
  166.5 0.0 reduce-scatter.2.cloned.1.call-update
  166.5 0.0 copy-done.1
  166.5 1.4 convolution_convert_fusion
  167.9 2.3 copy.24
  170.2 5.5 %all-to-all-done.1 = bf16[16,512,64]{1,2,0:T(8,128)(2,1)S(1)} async-done(((bf16[16,512,64]{1,2,0:T(8,128)(2,1)}), bf16[16,512,64]{1,2,0:T(8,128)(2,1)S(1)}, u32[]{:S(2)}, u32[]{:S(2)}) %all-to-all-start.1) | async-done | bytes 1048608 | tf_op jit(solution)/shard_map/all_to_all | solution.py:79
  175.8 1.0 copy-done
  176.7 6.1 %all-to-all-start.2 = ((bf16[16,64,1664]{2,1,0:T(8,128)(2,1)}), bf16[16,64,1664]{2,1,0:T(8,128)(2,1)S(1)}, u32[]{:S(2)}, u32[]{:S(2)}) async-start(bf16[16,64,1664]{2,1,0:T(8,128)(2,1)} %bitcast.107), calls=%async_computation.3 | async-start | bytes 6815744 | tf_op jit(solution)/shard_map/all_to_all | solution.py:80
  182.8 0.6 dynamic_slice.10
  183.4 0.1 dynamic_slice.11
  183.5 0.6 iota_compare_fusion.2
  184.2 0.9 constant_dynamic-slice_fusion
  185.1 1.8 fusion.10
  186.9 93.4 %psum.7 = bf16[32,64]{1,0:T(8,128)(2,1)S(1)} all-reduce(f32[32,64]{1,0:T(8,128)S(1)} %fusion.10), channel_id=1, replica_groups=mesh['req'=16,'tp'=32] {'tp'}, use_global_device_ids=true, to_apply=%region_3.4 | all-reduce | flops 2048 | bytes 12288 | tf_op jit(solution)/shard_map/psum | solution.py:90
  280.4 0.0 all-to-all-done.2
  280.4 1.0 reduce-scatter.2.cloned.1.call-done
  281.4 2.4 fusion.9
  (8 shorter events, 0.0 us)
Async XLA Ops:
  6.5 79.2 %all-gather.3.cloned.1.call-start = ((), (), s32[]{:S(2)}) async-start(), calls=%async_computation.5 | async-start | bytes 2162688 | tf_op jit(solution)/shard_map/all_gather | solution.py:42
  15.1 86.7 %copy-start.5 = (s32[512]{0:T(512)S(1)}, s32[512]{0:T(512)}, u32[]{:S(2)}) copy-start(s32[512]{0:T(512)} %param.13) | copy-start | bytes 6148
  15.1 127.0 %copy-start.4 = (bf16[8,1664]{1,0:T(8,128)(2,1)S(1)}, bf16[8,1664]{1,0:T(8,128)(2,1)}, u32[]{:S(2)}) copy-start(bf16[8,1664]{1,0:T(8,128)(2,1)} %param.10) | copy-start | bytes 79876
  15.1 127.0 %copy-start.3 = (bf16[4,512,64]{1,2,0:T(8,128)(2,1)S(1)}, bf16[4,512,64]{1,2,0:T(8,128)(2,1)}, u32[]{:S(2)}) copy-start(bf16[4,512,64]{1,2,0:T(8,128)(2,1)} %param.11) | copy-start | bytes 786436
  93.5 49.3 %copy-start.2 = (bf16[4,64,1664]{2,1,0:T(8,128)(2,1)S(1)}, bf16[4,64,1664]{2,1,0:T(8,128)(2,1)}, u32[]{:S(2)}) copy-start(bf16[4,64,1664]{2,1,0:T(8,128)(2,1)} %param.12) | copy-start | bytes 2555908
  94.6 58.9 %all-to-all-start = ((bf16[32,16,1024]{2,0,1:T(8,128)(2,1)}), bf16[32,16,1024]{2,0,1:T(8,128)(2,1)}, u32[]{:S(2)}, u32[]{:S(2)}) async-start(bf16[32,16,1024]{2,0,1:T(8,128)(2,1)} %bitcast.106), calls=%async_computation | async-start | bytes 2097152 | tf_op jit(solution)/shard_map/all_to_all | solution.py:43
  153.4 22.3 %all-to-all-start.1 = ((bf16[16,512,64]{1,2,0:T(8,128)(2,1)}), bf16[16,512,64]{1,2,0:T(8,128)(2,1)S(1)}, u32[]{:S(2)}, u32[]{:S(2)}) async-start(bf16[16,512,64]{1,2,0:T(8,128)(2,1)} %copy.20), calls=%async_computation.2 | async-start | bytes 2097152 | tf_op jit(solution)/shard_map/all_to_all | solution.py:79
  160.7 5.8 %copy-start.1 = (bf16[1,4,64,1664]{3,1,2,0:T(4,128)(2,1)S(1)}, bf16[1,4,64,1664]{3,1,2,0:T(4,128)(2,1)}, u32[]{:S(2)}) copy-start(bf16[1,4,64,1664]{3,1,2,0:T(4,128)(2,1)} %copy.23) | copy-start | bytes 2555908
  160.7 120.7 %reduce-scatter.2.cloned.1.call-start = ((), (), s32[]{:S(2)}) async-start(), calls=%async_computation.4 | async-start | bytes 1810432 | tf_op jit(solution)/shard_map/reduce_scatter | solution.py:93
  175.7 1.0 copy-start
  175.7 7.1 %copy-start.6 = (s32[16]{0:T(128)S(1)}, s32[16]{0:T(128)}, u32[]{:S(2)}) copy-start(s32[16]{0:T(128)} %param.15) | copy-start | bytes 196
  176.7 103.6 %all-to-all-start.2 = ((bf16[16,64,1664]{2,1,0:T(8,128)(2,1)}), bf16[16,64,1664]{2,1,0:T(8,128)(2,1)S(1)}, u32[]{:S(2)}, u32[]{:S(2)}) async-start(bf16[16,64,1664]{2,1,0:T(8,128)(2,1)} %bitcast.107), calls=%async_computation.3 | async-start | bytes 6815744 | tf_op jit(solution)/shard_map/all_to_all | solution.py:80
Sparse Core Ops, SparseCore 0:
  9.5 76.1 all-gather.2
  166.6 114.7 reduce-scatter.1
where the time goes:
time: 292 us; the launch traced here: 291 us
  blocking collectives  93.4 us (32%)
  waiting for transfers between devices  77.9 us (27%)
  other arithmetic  53.1 us (18%)
  starting transfers between devices  20.8 us (7%)
  local copies, waits for them, and re-layouts  20.1 us (7%)
  between operations  13.6 us (5%)
  matrix products  11.7 us (4%)
    psum x1, blocking collectives, body(): reduced = lax.psum(partial_low, 'tp').astype(jnp.bfloat16)  93.4 us
    all_gather x1, waiting for transfers between devices, body(): grouped = lax.all_gather(tokens, 'tp', axis=0, tiled=True)  70.6 us
    select_n x1, other arithmetic, body(): home_all = slots_all // per_home  40.2 us
    gather x5, local copies, waits for them, and re-layouts, body(): slots_all = adapter_slot[row_adapter]  7.91 us
    all_gather x1, other arithmetic, body(): grouped = lax.all_gather(tokens, 'tp', axis=0, tiled=True)  7.76 us
    all_to_all x1, starting transfers between devices, body(): lax.all_to_all(grouped.reshape(group_rows, home_count, block_width), 'req...  7.27 us
    all_to_all x1, starting transfers between devices, body(): lax.all_to_all(send_down, 'req', split_axis=0, concat_axis=0, tiled=True)  7.23 us
    all_to_all x1, starting transfers between devices, body(): lax.all_to_all(send_up, 'req', split_axis=0, concat_axis=0, tiled=True)  6.1 us
  transfers between devices with their start and end apart: 5, of which 3 were waited for; matrix products, arithmetic and copies ran while one was open for 25% of the time, Pallas kernels for 0%

commit v1 on v0

v1 whole, which is shorter than its diff:
```python
import functools

import jax
import jax.numpy as jnp
from jax import lax
from jax.experimental import pallas as pl
from jax.experimental.pallas import tpu as pltpu
from jax.sharding import PartitionSpec as P

MESH = pl.DeviceIdType.MESH
F32 = jnp.float32
BF16 = jnp.bfloat16
LANES = 128
SIDE = 4
HOMES = SIDE * SIDE
LAYERS = 16
HALF = HOMES // 2
adapter_scale = 2.0


def iota(shape, axis):
    return lax.broadcasted_iota(jnp.int32, shape, axis)


def ones_where(mask, dtype=BF16):
    return jnp.where(mask, 1.0, 0.0).astype(dtype)


def dot(a, b):
    return jnp.dot(a, b, preferred_element_type=F32)


def kernel(
    tok_hbm,
    codes_hbm,
    scales_hbm,
    down_hbm,
    up_hbm,
    row_ref,
    slot_ref,
    live_ref,
    out_ref,
    tok,
    codes,
    scales,
    down,
    up,
    mine,
    other,
    pairs,
    tiles,
    feats,
    onehot,
    wanted,
    packed,
    send_down,
    got_down,
    weight,
    shuffle,
    lhs,
    low_lhs,
    select,
    low_send,
    low_got,
    low_sum,
    low_sib,
    red_send,
    red,
    expand,
    spread,
    mask,
    total,
    part,
    got_part,
    half_sum,
    got_half,
    load_sem,
    sib_s,
    sib_r,
    blk_s,
    blk_r,
    slc_s,
    slc_r,
    dwn_s,
    dwn_r,
    zg1_s,
    zg1_r,
    zg2_s,
    zg2_r,
    zg3_s,
    zg3_r,
    low_s,
    low_r,
    red_s,
    red_r,
    rs1_s,
    rs1_r,
    rs2_s,
    rs2_r,
):
    g = lax.axis_index("req")
    t = lax.axis_index("tp")
    x, y = g // SIDE, g % SIDE
    z, c = t // 2, t % 2
    sib = (g, z * 2 + 1 - c)
    chunks = weight.shape[0]
    depth = weight.shape[1]
    groups = depth // LANES
    rank = down.shape[2]
    per_home = down.shape[0]
    adapters = HOMES * per_home
    group_rows = 2 * LAYERS
    lane_width = down.shape[1]
    half_width = lane_width // 2

    def plane(i):
        return lax.rem(x + i // SIDE, SIDE) * SIDE + lax.rem(y + i % SIDE, SIDE)

    def plane_from(i):
        return lax.rem(x + SIDE - i // SIDE, SIDE) * SIDE + lax.rem(y + SIDE - i % SIDE, SIDE)

    def layer(i):
        return lax.rem(z + i + LAYERS, LAYERS)

    def rcopy(src, dst, ss, rs, dev):
        return pltpu.make_async_remote_copy(
            src_ref=src, dst_ref=dst, send_sem=ss, recv_sem=rs, device_id=dev, device_id_type=MESH
        )

    def each(lo, hi, fn):
        def step(i, carry):
            fn(i)
            return carry

        lax.fori_loop(lo, hi, step, 0)

    barrier = pltpu.get_barrier_semaphore()

    def greet(i):
        pl.semaphore_signal(barrier, inc=1, device_id=(plane(i), t), device_id_type=MESH)
        pl.semaphore_signal(barrier, inc=1, device_id=(g, layer(i) * 2 + c), device_id_type=MESH)

    pl.semaphore_signal(barrier, inc=1, device_id=sib, device_id_type=MESH)
    each(1, HOMES, greet)

    loads = [
        pltpu.make_async_copy(src, dst, load_sem.at[i])
        for i, (src, dst) in enumerate(
            [(tok_hbm, tok), (down_hbm, down), (codes_hbm, codes), (scales_hbm, scales), (up_hbm, up)]
        )
    ]
    for load in loads:
        load.start()

    rows = row_ref[...]
    slots = jnp.zeros_like(rows)
    for a in range(adapters):
        slots = jnp.where(rows == a, slot_ref[a], slots)
    eye = ones_where(iota((adapters, adapters), 0) == iota((adapters, adapters), 1))
    for b in range(rows.shape[0]):
        hit = ones_where(slots[b : b + 1, :] == iota((adapters, LANES), 0))
        onehot[b * LANES : (b + 1) * LANES, :] = lax.dot_general(
            hit, eye, (((0,), (0,)), ((), ())), preferred_element_type=F32
        )
    all_rows = onehot.shape[0]
    in_group = ones_where(iota((HOMES, all_rows), 1) // group_rows == iota((HOMES, all_rows), 0))
    named = dot(in_group, onehot[...].astype(BF16))
    pick = ones_where(
        iota((adapters, per_home * LANES), 0) == g * per_home + iota((adapters, per_home * LANES), 1) // LANES
    )
    wanted[...] = jnp.where(dot(named.astype(BF16), pick) > 0, 1.0, 0.0)

    loads[0].wait()
    row = tok[...].astype(F32)
    for b in range(mine.shape[0] // 16):
        mine[b * 16 : (b + 1) * 16, :] = jnp.concatenate(
            [row[:, (b * 16 + i) * LANES : (b * 16 + i + 1) * LANES] for i in range(16)], axis=0
        ).astype(BF16)

    loads[1].wait()
    to_low = ones_where(iota((rank, LANES), 0) == iota((rank, LANES), 1))
    to_high = ones_where(iota((rank, LANES), 0) + rank == iota((rank, LANES), 1))
    for a in range(per_home):
        packed[a] = dot(down[a, :half_width, :], to_low) + dot(down[a, half_width:, :], to_high)

    def choose(b):
        weights = wanted[pl.ds(b, 1), :]
        block = packed[0] * weights[:, :LANES]
        for a in range(1, per_home):
            block += packed[a] * weights[:, a * LANES : (a + 1) * LANES]
        send_down[b] = block.astype(BF16)

    each(0, HOMES, choose)

    pl.semaphore_wait(barrier, 2 * (HOMES - 1) + 1)

    swap = rcopy(mine, other, sib_s.at[0], sib_r.at[0], sib)
    swap.start()
    swap.wait_recv()
    for b in range(HOMES // 2):
        own = mine[b * 16 : (b + 1) * 16, :].astype(F32)
        theirs = other[b * 16 : (b + 1) * 16, :].astype(F32)
        first = jnp.where(c == 0, own, theirs)
        second = jnp.where(c == 0, theirs, own)
        pairs[2 * b] = jnp.concatenate([first[:8], second[:8]], axis=0).astype(BF16)
        pairs[2 * b + 1] = jnp.concatenate([first[8:], second[8:]], axis=0).astype(BF16)

    carrier = g // HALF == c

    def block_copy(i):
        b = plane(i)
        return rcopy(pairs.at[b], tiles.at[c, z, g % HALF], blk_s.at[i], blk_r.at[i], (b, t))

    def slice_copy(i):
        d = layer(i)
        return rcopy(pairs.at[d], feats.at[z], slc_s.at[i], slc_r.at[i], (g, d * 2 + c))

    def down_copy(i):
        b = plane(i)
        return rcopy(send_down.at[b], got_down.at[g], dwn_s.at[i], dwn_r.at[i], (b, t))

    @pl.when(carrier)
    def _():
        each(1, HOMES, lambda i: block_copy(i).start())
        tiles[c, z, g % HALF] = pairs[g]

    each(1, LAYERS, lambda i: slice_copy(i).start())
    feats[z] = pairs[z]
    each(1, HOMES, lambda i: down_copy(i).start())
    got_down[g] = send_down[g]

    by_home = ones_where(iota((adapters, HOMES * LANES), 0) // per_home == iota((adapters, HOMES * LANES), 1) // LANES)
    select[...] = dot(onehot[pl.ds(pl.multiple_of(g * group_rows, group_rows), group_rows), :].astype(BF16), by_home)

    def place(b):
        return jnp.where(c == 0, b, (b % SIDE) * SIDE + b // SIDE)

    own_lanes = ones_where(
        iota((adapters, per_home * rank), 0) == g * per_home + iota((adapters, per_home * rank), 1) // rank
    )

    def own_mask(b):
        mask[pl.ds(pl.multiple_of(place(b) * group_rows, group_rows), group_rows), :] = dot(
            onehot[pl.ds(pl.multiple_of(b * group_rows, group_rows), group_rows), :].astype(BF16), own_lanes
        )

    loads[2].wait()
    loads[3].wait()

    def dequantize(k):
        cols = pl.ds(pl.multiple_of(k * LANES, LANES), LANES)
        scale = scales[:, cols].astype(F32)
        for j in range(groups):
            weight[k, j * LANES : (j + 1) * LANES, :] = (
                codes[j * LANES : (j + 1) * LANES, cols].astype(F32) * scale[j : j + 1, :]
            ).astype(BF16)

    each(0, chunks // 2, dequantize)

    def wait_block(i):
        @pl.when(plane_from(i) // HALF == c)
        def _():
            block_copy(i).wait_recv()

    each(1, HOMES, wait_block)

    far = (3, -3, 6, -6)

    def far_copy(n):
        return rcopy(
            tiles.at[c, z], tiles.at[c, z], zg1_s.at[n], zg1_r.at[n], (g, layer(far[n]) * 2 + c)
        )

    near = [(src, step) for src in (0, -3, 3, -6, 6) for step in (1, -1)]

    def near_copy(n):
        src, step = near[n]
        s = layer(src)
        return rcopy(tiles.at[c, s], tiles.at[c, s], zg2_s.at[n], zg2_r.at[n], (g, layer(step) * 2 + c))

    quarter = HALF // 2

    def last_copy(n):
        src, step = ((-6, 2), (6, -2))[n]
        s = layer(src)
        some = tiles.at[c, s, pl.ds(n * quarter, quarter)]
        return rcopy(some, some, zg3_s.at[n], zg3_r.at[n], (g, layer(step) * 2 + c))

    for n in range(4):
        far_copy(n).start()
    for n in range(2):
        near_copy(n).start()

    each(chunks // 2, chunks, dequantize)
    each(0, HOMES, own_mask)

    each(1, LAYERS, lambda i: slice_copy(i).wait_recv())
    shuffle[...] = feats[...].astype(F32).reshape(LAYERS * 16, LANES)
    for j in range(lane_width // LANES):
        low_lhs[:, j * LANES : (j + 1) * LANES] = shuffle[
            pl.ds(c * (lane_width // LANES) + j, group_rows, stride=8), :
        ].astype(BF16)

    each(1, HOMES, lambda i: down_copy(i).wait_recv())
    first = jnp.zeros((group_rows, LANES), F32)
    second = jnp.zeros((group_rows, LANES), F32)
    for b in range(HOMES):
        here = select[:, b * LANES : (b + 1) * LANES]
        first += here * dot(low_lhs[:, :half_width], got_down[b])
        second += here * dot(low_lhs[:, half_width:], got_down[b])
    reduced = first + pltpu.roll(second, rank, 1)
    low = jnp.where(
        iota((LAYERS, LANES), 1) < rank, reduced[:LAYERS], pltpu.roll(reduced[LAYERS:], rank, 1)
    )
    low_sum[...] = low
    low_send[...] = low.astype(BF16)

    def low_copy(i):
        return rcopy(low_send, low_got.at[z], low_s.at[i], low_r.at[i], (g, layer(i) * 2 + c))

    each(1, LAYERS, lambda i: low_copy(i).start())

    for n, come in enumerate((-3, 3, -6, 6)):
        far_copy(n).wait_recv()
        near_copy(2 + 2 * n).start()
        near_copy(3 + 2 * n).start()
    last_copy(0).start()
    last_copy(1).start()

    low_got[z] = jnp.zeros((LAYERS, LANES), BF16)
    each(1, LAYERS, lambda i: low_copy(i).wait_recv())
    acc = low_sum[...]
    for b in range(LAYERS):
        acc += low_got[b].astype(F32)
    low_sum[...] = acc
    swap_low = rcopy(low_sum, low_sib, sib_s.at[1], sib_r.at[1], sib)
    swap_low.start()
    swap_low.wait_recv()
    red_send[...] = (low_sum[...] + low_sib[...]).astype(BF16)

    def red_copy(i):
        return rcopy(red_send, red.at[g], red_s.at[i], red_r.at[i], (plane(i), t))

    each(1, HOMES, lambda i: red_copy(i).start())
    red[g] = red_send[...]

    for n in range(len(near)):
        near_copy(n).wait_recv()
    last_copy(0).wait_recv()
    last_copy(1).wait_recv()
    swap_tiles = rcopy(tiles.at[c], tiles.at[c], sib_s.at[2], sib_r.at[2], sib)
    swap_tiles.start()
    swap_tiles.wait_recv()

    def arrange(b):
        shuffle[...] = tiles[b // HALF, :, b % HALF].astype(F32).reshape(LAYERS * 16, LANES)
        here = pl.ds(pl.multiple_of(place(b) * group_rows, group_rows), group_rows)
        for j in range(groups):
            lhs[here, j * LANES : (j + 1) * LANES] = shuffle[pl.ds(j, group_rows, stride=8), :].astype(BF16)

    each(0, HOMES, arrange)

    def base(k):
        total[k] = dot(lhs[...], weight[k])

    each(0, chunks, base)

    each(1, HOMES, lambda i: red_copy(i).wait_recv())
    spread_from = iota((LANES, 2 * per_home * rank), 0)
    spread_to = iota((LANES, 2 * per_home * rank), 1)
    copies = ones_where(
        spread_from == spread_to % rank + (spread_to // (per_home * rank)) * rank
    )
    wide = per_home * rank
    expand[...] = dot(red[...].reshape(HOMES * LAYERS, LANES), copies)
    for b in range(HOMES):
        here = pl.multiple_of(place(b) * group_rows, group_rows)
        lines = expand[b * LAYERS : (b + 1) * LAYERS, :]
        top = pl.ds(here, LAYERS)
        bottom = pl.ds(pl.multiple_of(here + LAYERS, LAYERS), LAYERS)
        spread[top, :] = (lines[:, :wide] * mask[top, :]).astype(BF16)
        spread[bottom, :] = (lines[:, wide:] * mask[bottom, :]).astype(BF16)

    loads[4].wait()
    first_at = jnp.where(c == 0, x, y)
    second_at = jnp.where(c == 0, y, x)
    four = SIDE * group_rows

    def along_first(d):
        to = lax.rem(first_at + d, SIDE)
        return to, (jnp.where(c == 0, to * SIDE + y, x * SIDE + to), t)

    def along_second(d):
        to = lax.rem(second_at + d, SIDE)
        return to, (jnp.where(c == 0, x * SIDE + to, to * SIDE + y), t)

    def part_copy(k, d):
        to, dev = along_first(d)
        src = part.at[k, pl.ds(pl.multiple_of(to * four, four), four)]
        return rcopy(src, got_part.at[k, d - 1], rs1_s.at[k, d - 1], rs1_r.at[k, d - 1], dev)

    def half_copy(k, d):
        to, dev = along_second(d)
        src = half_sum.at[k, pl.ds(pl.multiple_of(to * group_rows, group_rows), group_rows)]
        return rcopy(src, got_half.at[k, d - 1], rs2_s.at[k, d - 1], rs2_r.at[k, d - 1], dev)

    def send_part(k):
        cols = pl.ds(pl.multiple_of(k * LANES, LANES), LANES)
        part[k] = (total[k] + adapter_scale * dot(spread[...], up[:, cols])).astype(BF16)
        for d in range(1, SIDE):
            part_copy(k, d).start()

    each(0, chunks, send_part)

    def send_half(k):
        own = part[k, pl.ds(pl.multiple_of(first_at * four, four), four), :].astype(F32)
        for d in range(1, SIDE):
            part_copy(k, d).wait_recv()
            own += got_part[k, d - 1].astype(F32)
        half_sum[k] = own.astype(BF16)
        for d in range(1, SIDE):
            half_copy(k, d).start()

    each(0, chunks, send_half)

    live = iota((group_rows, LANES), 0) < live_ref[g]

    def finish(k):
        own = half_sum[k, pl.ds(pl.multiple_of(second_at * group_rows, group_rows), group_rows), :].astype(F32)
        for d in range(1, SIDE):
            half_copy(k, d).wait_recv()
            own += got_half[k, d - 1].astype(F32)
        out_ref[:, pl.ds(pl.multiple_of(k * LANES, LANES), LANES)] = jnp.where(live, own, 0.0).astype(BF16)

    each(0, chunks, finish)

    swap.wait_send()
    swap_low.wait_send()
    swap_tiles.wait_send()

    @pl.when(carrier)
    def _():
        each(1, HOMES, lambda i: block_copy(i).wait_send())

    def sent(i):
        slice_copy(i).wait_send()
        down_copy(i).wait_send()
        low_copy(i).wait_send()
        red_copy(i).wait_send()

    each(1, HOMES, sent)
    for n in range(4):
        far_copy(n).wait_send()
    for n in range(len(near)):
        near_copy(n).wait_send()
    last_copy(0).wait_send()
    last_copy(1).wait_send()

    def sent_parts(k):
        for d in range(1, SIDE):
            part_copy(k, d).wait_send()
            half_copy(k, d).wait_send()

    each(0, chunks, sent_parts)


def body(tokens, weight_codes, weight_scales, adapter_down, adapter_up, row_adapter, adapter_slot, live_rows):
    width = tokens.shape[1]
    depth, columns = weight_codes.shape
    per_home, lane_width, rank = adapter_down.shape
    all_rows = row_adapter.shape[0]
    group_rows = all_rows // HOMES
    chunks = columns // LANES
    wide = per_home * rank
    up = adapter_up.reshape(wide, columns)
    rows = row_adapter.reshape(all_rows // LANES, LANES)
    vmem, dma = pltpu.VMEM, pltpu.SemaphoreType.DMA
    scratch = [
        vmem((1, width), BF16),
        vmem((depth, columns), BF16),
        vmem(weight_scales.shape, BF16),
        vmem(adapter_down.shape, BF16),
        vmem((wide, columns), BF16),
        vmem((width // LANES, LANES), BF16),
        vmem((width // LANES, LANES), BF16),
        vmem((HOMES, 16, LANES), BF16),
        vmem((2, LAYERS, HALF, 16, LANES), BF16),
        vmem((LAYERS, 16, LANES), BF16),
        vmem((all_rows, HOMES * per_home), F32),
        vmem((HOMES, per_home * LANES), F32),
        vmem((per_home, lane_width // 2, LANES), F32),
        vmem((HOMES, lane_width // 2, LANES), BF16),
        vmem((HOMES, lane_width // 2, LANES), BF16),
        vmem((chunks, depth, LANES), BF16),
        vmem((LAYERS * 16, LANES), F32),
        vmem((all_rows, depth), BF16),
        vmem((group_rows, lane_width), BF16),
        vmem((group_rows, HOMES * LANES), F32),
        vmem((LAYERS, LANES), BF16),
        vmem((LAYERS, LAYERS, LANES), BF16),
        vmem((LAYERS, LANES), F32),
        vmem((LAYERS, LANES), F32),
        vmem((LAYERS, LANES), BF16),
        vmem((HOMES, LAYERS, LANES), BF16),
        vmem((HOMES * LAYERS, 2 * wide), F32),
        vmem((all_rows, wide), BF16),
        vmem((all_rows, wide), F32),
        vmem((chunks, all_rows, LANES), F32),
        vmem((chunks, all_rows, LANES), BF16),
        vmem((chunks, SIDE - 1, SIDE * group_rows, LANES), BF16),
        vmem((chunks, SIDE * group_rows, LANES), BF16),
        vmem((chunks, SIDE - 1, group_rows, LANES), BF16),
        dma((5,)),
        dma((3,)),
        dma((3,)),
    ]
    for count in (HOMES, LAYERS, HOMES, 4, 10, 2, LAYERS, HOMES):
        scratch += [dma((count,)), dma((count,))]
    scratch += [dma((chunks, SIDE - 1))] * 4
    return pl.pallas_call(
        kernel,
        out_shape=jax.ShapeDtypeStruct((group_rows, columns), BF16),
        in_specs=[pl.BlockSpec(memory_space=pl.ANY)] * 5
        + [pl.BlockSpec(memory_space=pltpu.VMEM)]
        + [pl.BlockSpec(memory_space=pltpu.SMEM)] * 2,
        out_specs=pl.BlockSpec(memory_space=pltpu.VMEM),
        scratch_shapes=scratch,
        compiler_params=pltpu.CompilerParams(
            collective_id=0, has_side_effects=True, vmem_limit_bytes=48 * 1024 * 1024
        ),
    )(tokens, weight_codes, weight_scales, adapter_down, up, rows, adapter_slot, live_rows)


def solution(mesh):
    in_specs = (
        P(("req", "tp"), None),
        P("req", "tp"),
        P("req", "tp"),
        P("req", "tp", None),
        P("req", None, "tp"),
        P(),
        P(),
        P(),
    )
    return jax.shard_map(body, mesh=mesh, in_specs=in_specs, out_specs=P("req", "tp"), check_vma=False)
```

time: 292 us -> 84.4 us (0.29)
  the two profiles are of different devices: /device:TPU:6 before, /device:TPU:8 now
where the time goes in v1:
time: 84.4 us; the launch traced here: 84 us
  Pallas kernels  75.4 us (89%)
  local copies, waits for them, and re-layouts  8.55 us (10%)
    pallas_call x1, Pallas kernels, body(): pl.pallas_call(kernel, out_shape=jax.ShapeDtypeStruct((group_rows, column...  75.4 us
    unnamed x16, local copies, waits for them, and re-layouts  8.55 us

profile of v1, /device:TPU:8, one launch (start us, length us, event | category | flops | bytes accessed | tf_op | source)
XLA Modules:
  0.0 84.0 jit_solution(13517417301564634136)
XLA Ops:
  0.0 1.2 %copy.9.down_hbm = bf16[4,512,64]{2,1,0:T(8,128)(2,1)S(1)} copy(bf16[4,512,64]{1,2,0:T(8,128)(2,1)} %param.11) | data formatting | bytes 524288 | tf_op args[3]
  1.2 0.0 copy-start
  1.2 2.0 %copy-done = bf16[1024,1664]{1,0:T(8,128)(2,1)S(1)} copy-done((bf16[1024,1664]{1,0:T(8,128)(2,1)S(1)}, bf16[1024,1664]{1,0:T(8,128)(2,1)}, u32[]{:S(2)}) %copy-start) | copy-done | bytes 3407896
  3.2 0.0 copy-start.1
  3.2 1.2 %copy-done.1 = bf16[4,64,1664]{2,1,0:T(8,128)(2,1)S(1)} copy-done((bf16[4,64,1664]{2,1,0:T(8,128)(2,1)S(1)}, bf16[4,64,1664]{2,1,0:T(8,128)(2,1)}, u32[]{:S(2)}) %copy-start.1) | copy-done | bytes 851992
  4.4 0.0 copy-start.2
  4.4 0.8 copy-done.2
  5.2 0.0 copy-start.3
  5.2 0.7 copy-done.3
  5.9 0.0 copy-start.4
  5.9 0.7 copy-done.4
  6.6 0.0 copy-start.5
  6.6 0.7 copy-done.5
  7.3 0.0 copy-start.6
  7.3 0.7 copy-done.6
  7.9 75.4 %shard_map.82 = bf16[32,1664]{1,0:T(8,128)(2,1)S(1)} custom-call(bf16[1,16384]{1,0:T(2,128)(2,1)S(1)} %copy-done.2, bf16[1024,1664]{1,0:T(8,128)(2,1)S(1)} %copy-done, bf16[8,1664]{1,0:T(8,128)(2,1)S(1)} %copy-done.3, bf16[4,512,64]{2,1,0:T(8,128)(2,1)S(1)} %copy.9.down_hbm, bf16[256,1664]{1,0:T(8,128)(2,1)S(1)} %bitcast.2, s32[4,128]{1,0:T(4,128)S(1)} %bitcast.3, ...), custom_call_target="tpu_custom_call" | custom-call | tf_op jit(solution)/shard_map/pallas_call | solution.py:520
  83.4 0.6 copy.11
Async XLA Ops:
  1.2 2.0 %copy-start = (bf16[1024,1664]{1,0:T(8,128)(2,1)S(1)}, bf16[1024,1664]{1,0:T(8,128)(2,1)}, u32[]{:S(2)}) copy-start(bf16[1024,1664]{1,0:T(8,128)(2,1)} %codes_hbm.1) | copy-start | bytes 10223620
  3.2 1.2 %copy-start.1 = (bf16[4,64,1664]{2,1,0:T(8,128)(2,1)S(1)}, bf16[4,64,1664]{2,1,0:T(8,128)(2,1)}, u32[]{:S(2)}) copy-start(bf16[4,64,1664]{2,1,0:T(8,128)(2,1)} %param.12) | copy-start | bytes 2555908
  4.4 0.8 copy-start.2
  5.2 0.7 copy-start.3
  5.9 0.7 copy-start.4
  6.6 0.7 copy-start.5
  7.3 0.7 copy-start.6

commit v2 on v1

--- a/solution.py
+++ b/solution.py
@@ -36,10 +36,13 @@
     scales_hbm,
     down_hbm,
     up_hbm,
+    row_hbm,
+    slot_hbm,
+    live_hbm,
+    out_ref,
     row_ref,
     slot_ref,
     live_ref,
-    out_ref,
     tok,
     codes,
     scales,
@@ -52,7 +55,6 @@
     feats,
     onehot,
     wanted,
-    packed,
     send_down,
     got_down,
     weight,
@@ -89,6 +91,8 @@
     zg2_r,
     zg3_s,
     zg3_r,
+    pas_s,
+    pas_r,
     low_s,
     low_r,
     red_s,
@@ -103,15 +107,12 @@
     x, y = g // SIDE, g % SIDE
     z, c = t // 2, t % 2
     sib = (g, z * 2 + 1 - c)
-    chunks = weight.shape[0]
-    depth = weight.shape[1]
+    depth, columns = weight.shape
+    chunks = columns // LANES
     groups = depth // LANES
-    rank = down.shape[2]
-    per_home = down.shape[0]
+    per_home, rank, lane_width = down.shape
     adapters = HOMES * per_home
     group_rows = 2 * LAYERS
-    lane_width = down.shape[1]
-    half_width = lane_width // 2
 
     def plane(i):
         return lax.rem(x + i // SIDE, SIDE) * SIDE + lax.rem(y + i % SIDE, SIDE)
@@ -127,6 +128,14 @@
             src_ref=src, dst_ref=dst, send_sem=ss, recv_sem=rs, device_id=dev, device_id_type=MESH
         )
 
+    early = 4
+    across = (10, 9, 11, 6, 14, 5, 7, 13, 15, 8, 2, 1, 3, 4, 12)
+    along = (8, 7, 9, 6, 10, 5, 11, 4, 12, 3, 13, 2, 14, 1, 15)
+
+    def in_order(order, fn):
+        for i in order:
+            fn(i)
+
     def each(lo, hi, fn):
         def step(i, carry):
             fn(i)
@@ -146,12 +155,30 @@
     loads = [
         pltpu.make_async_copy(src, dst, load_sem.at[i])
         for i, (src, dst) in enumerate(
-            [(tok_hbm, tok), (down_hbm, down), (codes_hbm, codes), (scales_hbm, scales), (up_hbm, up)]
+            [
+                (tok_hbm, tok),
+                (down_hbm, down),
+                (codes_hbm, codes),
+                (scales_hbm, scales),
+                (up_hbm, up),
+                (row_hbm, row_ref),
+                (slot_hbm, slot_ref),
+                (live_hbm, live_ref),
+            ]
         )
     ]
-    for load in loads:
-        load.start()
-
+    for i in (5, 6, 1, 0, 2, 3, 4, 7):
+        loads[i].start()
+
+    loads[0].wait()
+    row = tok[...].astype(F32)
+    for b in range(mine.shape[0] // 16):
+        mine[b * 16 : (b + 1) * 16, :] = jnp.concatenate(
+            [row[:, (b * 16 + i) * LANES : (b * 16 + i + 1) * LANES] for i in range(16)], axis=0
+        ).astype(BF16)
+
+    loads[5].wait()
+    loads[6].wait()
     rows = row_ref[...]
     slots = jnp.zeros_like(rows)
     for a in range(adapters):
@@ -166,36 +193,37 @@
     in_group = ones_where(iota((HOMES, all_rows), 1) // group_rows == iota((HOMES, all_rows), 0))
     named = dot(in_group, onehot[...].astype(BF16))
     pick = ones_where(
-        iota((adapters, per_home * LANES), 0) == g * per_home + iota((adapters, per_home * LANES), 1) // LANES
+        iota((adapters, per_home * lane_width), 0)
+        == g * per_home + iota((adapters, per_home * lane_width), 1) // lane_width
     )
     wanted[...] = jnp.where(dot(named.astype(BF16), pick) > 0, 1.0, 0.0)
 
-    loads[0].wait()
-    row = tok[...].astype(F32)
-    for b in range(mine.shape[0] // 16):
-        mine[b * 16 : (b + 1) * 16, :] = jnp.concatenate(
-            [row[:, (b * 16 + i) * LANES : (b * 16 + i + 1) * LANES] for i in range(16)], axis=0
-        ).astype(BF16)
-
     loads[1].wait()
-    to_low = ones_where(iota((rank, LANES), 0) == iota((rank, LANES), 1))
-    to_high = ones_where(iota((rank, LANES), 0) + rank == iota((rank, LANES), 1))
-    for a in range(per_home):
-        packed[a] = dot(down[a, :half_width, :], to_low) + dot(down[a, half_width:, :], to_high)
 
     def choose(b):
-        weights = wanted[pl.ds(b, 1), :]
-        block = packed[0] * weights[:, :LANES]
-        for a in range(1, per_home):
-            block += packed[a] * weights[:, a * LANES : (a + 1) * LANES]
-        send_down[b] = block.astype(BF16)
+        line = wanted[pl.ds(b, 1), :]
+        weights = [
+            jnp.broadcast_to(line[:, a * lane_width : (a + 1) * lane_width], (16, lane_width)).astype(BF16)
+            for a in range(per_home)
+        ]
+        for i in range(rank // 16):
+            lines = slice(i * 16, (i + 1) * 16)
+            block = down[0, lines, :] * weights[0]
+            for a in range(1, per_home):
+                block += down[a, lines, :] * weights[a]
+            send_down[b, lines, :] = block
 
     each(0, HOMES, choose)
 
     pl.semaphore_wait(barrier, 2 * (HOMES - 1) + 1)
+
+    def down_copy(i):
+        b = plane(i)
+        return rcopy(send_down.at[b], got_down.at[g], dwn_s.at[i], dwn_r.at[i], (b, t))
 
     swap = rcopy(mine, other, sib_s.at[0], sib_r.at[0], sib)
     swap.start()
+    in_order(across[:early], lambda i: down_copy(i).start())
     swap.wait_recv()
     for b in range(HOMES // 2):
         own = mine[b * 16 : (b + 1) * 16, :].astype(F32)
@@ -215,21 +243,17 @@
         d = layer(i)
         return rcopy(pairs.at[d], feats.at[z], slc_s.at[i], slc_r.at[i], (g, d * 2 + c))
 
-    def down_copy(i):
-        b = plane(i)
-        return rcopy(send_down.at[b], got_down.at[g], dwn_s.at[i], dwn_r.at[i], (b, t))
-
     @pl.when(carrier)
     def _():
-        each(1, HOMES, lambda i: block_copy(i).start())
+        in_order(across, lambda i: block_copy(i).start())
         tiles[c, z, g % HALF] = pairs[g]
 
-    each(1, LAYERS, lambda i: slice_copy(i).start())
+    in_order(along, lambda i: slice_copy(i).start())
     feats[z] = pairs[z]
-    each(1, HOMES, lambda i: down_copy(i).start())
+    in_order(across[early:], lambda i: down_copy(i).start())
     got_down[g] = send_down[g]
 
-    by_home = ones_where(iota((adapters, HOMES * LANES), 0) // per_home == iota((adapters, HOMES * LANES), 1) // LANES)
+    by_home = ones_where(iota((adapters, HOMES * rank), 0) // per_home == iota((adapters, HOMES * rank), 1) // rank)
     select[...] = dot(onehot[pl.ds(pl.multiple_of(g * group_rows, group_rows), group_rows), :].astype(BF16), by_home)
 
     def place(b):
@@ -251,7 +275,7 @@
         cols = pl.ds(pl.multiple_of(k * LANES, LANES), LANES)
         scale = scales[:, cols].astype(F32)
         for j in range(groups):
-            weight[k, j * LANES : (j + 1) * LANES, :] = (
+            weight[j * LANES : (j + 1) * LANES, cols] = (
                 codes[j * LANES : (j + 1) * LANES, cols].astype(F32) * scale[j : j + 1, :]
             ).astype(BF16)
 
@@ -264,14 +288,14 @@
 
     each(1, HOMES, wait_block)
 
-    far = (3, -3, 6, -6)
+    far = (6, -6, 3, -3)
 
     def far_copy(n):
         return rcopy(
             tiles.at[c, z], tiles.at[c, z], zg1_s.at[n], zg1_r.at[n], (g, layer(far[n]) * 2 + c)
         )
 
-    near = [(src, step) for src in (0, -3, 3, -6, 6) for step in (1, -1)]
+    near = [(src, step) for src in (0, -6, 6, -3, 3) for step in (1, -1)]
 
     def near_copy(n):
         src, step = near[n]
@@ -286,10 +310,17 @@
         some = tiles.at[c, s, pl.ds(n * quarter, quarter)]
         return rcopy(some, some, zg3_s.at[n], zg3_r.at[n], (g, layer(step) * 2 + c))
 
+    begun = [0] + [-d for d in far] + [src - step for src, step in near] + [8]
+
+    def pass_copy(n):
+        some = tiles.at[c, layer(begun[n])]
+        return rcopy(some, some, pas_s.at[n], pas_r.at[n], sib)
+
     for n in range(4):
         far_copy(n).start()
     for n in range(2):
         near_copy(n).start()
+    pass_copy(0).start()
 
     each(chunks // 2, chunks, dequantize)
     each(0, HOMES, own_mask)
@@ -302,30 +333,32 @@
         ].astype(BF16)
 
     each(1, HOMES, lambda i: down_copy(i).wait_recv())
-    first = jnp.zeros((group_rows, LANES), F32)
-    second = jnp.zeros((group_rows, LANES), F32)
-    for b in range(HOMES):
-        here = select[:, b * LANES : (b + 1) * LANES]
-        first += here * dot(low_lhs[:, :half_width], got_down[b])
-        second += here * dot(low_lhs[:, half_width:], got_down[b])
-    reduced = first + pltpu.roll(second, rank, 1)
-    low = jnp.where(
-        iota((LAYERS, LANES), 1) < rank, reduced[:LAYERS], pltpu.roll(reduced[LAYERS:], rank, 1)
+    chosen = select[...] * lax.dot_general(
+        low_lhs[...],
+        got_down[...].reshape(HOMES * rank, lane_width),
+        (((1,), (1,)), ((), ())),
+        preferred_element_type=F32,
     )
+    reduced = chosen[:, :LANES]
+    for b in range(1, HOMES * rank // LANES):
+        reduced += chosen[:, b * LANES : (b + 1) * LANES]
+    reduced += pltpu.roll(reduced, rank, 1)
+    low = jnp.where(iota((LAYERS, LANES), 1) < rank, reduced[:LAYERS], reduced[LAYERS:])
     low_sum[...] = low
     low_send[...] = low.astype(BF16)
 
     def low_copy(i):
         return rcopy(low_send, low_got.at[z], low_s.at[i], low_r.at[i], (g, layer(i) * 2 + c))
 
-    each(1, LAYERS, lambda i: low_copy(i).start())
-
-    for n, come in enumerate((-3, 3, -6, 6)):
+    in_order(along, lambda i: low_copy(i).start())
+
+    for n in range(4):
         far_copy(n).wait_recv()
         near_copy(2 + 2 * n).start()
         near_copy(3 + 2 * n).start()
-    last_copy(0).start()
-    last_copy(1).start()
+        if n < 2:
+            last_copy(n).start()
+        pass_copy(1 + n).start()
 
     low_got[z] = jnp.zeros((LAYERS, LANES), BF16)
     each(1, LAYERS, lambda i: low_copy(i).wait_recv())
@@ -341,16 +374,18 @@
     def red_copy(i):
         return rcopy(red_send, red.at[g], red_s.at[i], red_r.at[i], (plane(i), t))
 
-    each(1, HOMES, lambda i: red_copy(i).start())
+    in_order(across, lambda i: red_copy(i).start())
     red[g] = red_send[...]
 
     for n in range(len(near)):
         near_copy(n).wait_recv()
+        pass_copy(5 + n).start()
     last_copy(0).wait_recv()
     last_copy(1).wait_recv()
-    swap_tiles = rcopy(tiles.at[c], tiles.at[c], sib_s.at[2], sib_r.at[2], sib)
-    swap_tiles.start()
-    swap_tiles.wait_recv()
+    pass_copy(15).start()
+
+    for n in range(LAYERS):
+        pass_copy(n).wait_recv()
 
     def arrange(b):
         shuffle[...] = tiles[b // HALF, :, b % HALF].astype(F32).reshape(LAYERS * 16, LANES)
@@ -360,10 +395,14 @@
 
     each(0, HOMES, arrange)
 
-    def base(k):
-        total[k] = dot(lhs[...], weight[k])
-
-    each(0, chunks, base)
+    def base(k, width):
+        block = dot(lhs[...], weight[:, pl.ds(pl.multiple_of(k * LANES, LANES), width)])
+        for i in range(width // LANES):
+            total[k + i] = block[:, i * LANES : (i + 1) * LANES]
+
+    each(0, chunks // 2, lambda n: base(2 * n, 2 * LANES))
+    if chunks % 2:
+        base(chunks - 1, LANES)
 
     each(1, HOMES, lambda i: red_copy(i).wait_recv())
     spread_from = iota((LANES, 2 * per_home * rank), 0)
@@ -404,13 +443,12 @@
         src = half_sum.at[k, pl.ds(pl.multiple_of(to * group_rows, group_rows), group_rows)]
         return rcopy(src, got_half.at[k, d - 1], rs2_s.at[k, d - 1], rs2_r.at[k, d - 1], dev)
 
-    def send_part(k):
-        cols = pl.ds(pl.multiple_of(k * LANES, LANES), LANES)
-        part[k] = (total[k] + adapter_scale * dot(spread[...], up[:, cols])).astype(BF16)
-        for d in range(1, SIDE):
-            part_copy(k, d).start()
-
-    each(0, chunks, send_part)
+    def send_part(k, width):
+        block = dot(spread[...], up[:, pl.ds(pl.multiple_of(k * LANES, LANES), width)])
+        for i in range(width // LANES):
+            part[k + i] = (total[k + i] + adapter_scale * block[:, i * LANES : (i + 1) * LANES]).astype(BF16)
+            for d in range(1, SIDE):
+                part_copy(k + i, d).start()
 
     def send_half(k):
         own = part[k, pl.ds(pl.multiple_of(first_at * four, four), four), :].astype(F32)
@@ -421,8 +459,20 @@
         for d in range(1, SIDE):
             half_copy(k, d).start()
 
-    each(0, chunks, send_half)
-
+    lead = 4
+
+    def both(n):
+        send_part(2 * n + lead, 2 * LANES)
+        send_half(2 * n)
+        send_half(2 * n + 1)
+
+    each(0, lead // 2, lambda n: send_part(2 * n, 2 * LANES))
+    each(0, (chunks - lead) // 2, both)
+    if chunks % 2:
+        send_part(chunks - 1, LANES)
+    each((chunks - lead) // 2 * 2, chunks, send_half)
+
+    loads[7].wait()
     live = iota((group_rows, LANES), 0) < live_ref[g]
 
     def finish(k):
@@ -436,7 +486,6 @@
 
     swap.wait_send()
     swap_low.wait_send()
-    swap_tiles.wait_send()
 
     @pl.when(carrier)
     def _():
@@ -455,6 +504,8 @@
         near_copy(n).wait_send()
     last_copy(0).wait_send()
     last_copy(1).wait_send()
+    for n in range(LAYERS):
+        pass_copy(n).wait_send()
 
     def sent_parts(k):
         for d in range(1, SIDE):
@@ -467,7 +518,8 @@
 def body(tokens, weight_codes, weight_scales, adapter_down, adapter_up, row_adapter, adapter_slot, live_rows):
     width = tokens.shape[1]
     depth, columns = weight_codes.shape
-    per_home, lane_width, rank = adapter_down.shape
+    down = jnp.swapaxes(adapter_down, 1, 2)
+    per_home, rank, lane_width = down.shape
     all_rows = row_adapter.shape[0]
     group_rows = all_rows // HOMES
     chunks = columns // LANES
@@ -476,10 +528,13 @@
     rows = row_adapter.reshape(all_rows // LANES, LANES)
     vmem, dma = pltpu.VMEM, pltpu.SemaphoreType.DMA
     scratch = [
+        vmem(rows.shape, jnp.int32),
+        pltpu.SMEM(adapter_slot.shape, jnp.int32),
+        pltpu.SMEM(live_rows.shape, jnp.int32),
         vmem((1, width), BF16),
         vmem((depth, columns), BF16),
         vmem(weight_scales.shape, BF16),
-        vmem(adapter_down.shape, BF16),
+        vmem(down.shape, BF16),
         vmem((wide, columns), BF16),
         vmem((width // LANES, LANES), BF16),
         vmem((width // LANES, LANES), BF16),
@@ -487,15 +542,14 @@
         vmem((2, LAYERS, HALF, 16, LANES), BF16),
         vmem((LAYERS, 16, LANES), BF16),
         vmem((all_rows, HOMES * per_home), F32),
-        vmem((HOMES, per_home * LANES), F32),
-        vmem((per_home, lane_width // 2, LANES), F32),
-        vmem((HOMES, lane_width // 2, LANES), BF16),
-        vmem((HOMES, lane_width // 2, LANES), BF16),
-        vmem((chunks, depth, LANES), BF16),
+        vmem((HOMES, per_home * lane_width), F32),
+        vmem((HOMES, rank, lane_width), BF16),
+        vmem((HOMES, rank, lane_width), BF16),
+        vmem((depth, columns), BF16),
         vmem((LAYERS * 16, LANES), F32),
         vmem((all_rows, depth), BF16),
         vmem((group_rows, lane_width), BF16),
-        vmem((group_rows, HOMES * LANES), F32),
+        vmem((group_rows, HOMES * rank), F32),
         vmem((LAYERS, LANES), BF16),
         vmem((LAYERS, LAYERS, LANES), BF16),
         vmem((LAYERS, LANES), F32),
@@ -510,25 +564,23 @@
         vmem((chunks, SIDE - 1, SIDE * group_rows, LANES), BF16),
         vmem((chunks, SIDE * group_rows, LANES), BF16),
         vmem((chunks, SIDE - 1, group_rows, LANES), BF16),
-        dma((5,)),
+        dma((8,)),
         dma((3,)),
         dma((3,)),
     ]
-    for count in (HOMES, LAYERS, HOMES, 4, 10, 2, LAYERS, HOMES):
+    for count in (HOMES, LAYERS, HOMES, 4, 10, 2, LAYERS, LAYERS, HOMES):
         scratch += [dma((count,)), dma((count,))]
     scratch += [dma((chunks, SIDE - 1))] * 4
     return pl.pallas_call(
         kernel,
         out_shape=jax.ShapeDtypeStruct((group_rows, columns), BF16),
-        in_specs=[pl.BlockSpec(memory_space=pl.ANY)] * 5
-        + [pl.BlockSpec(memory_space=pltpu.VMEM)]
-        + [pl.BlockSpec(memory_space=pltpu.SMEM)] * 2,
+        in_specs=[pl.BlockSpec(memory_space=pltpu.HBM)] * 8,
         out_specs=pl.BlockSpec(memory_space=pltpu.VMEM),
         scratch_shapes=scratch,
         compiler_params=pltpu.CompilerParams(
-            collective_id=0, has_side_effects=True, vmem_limit_bytes=48 * 1024 * 1024
+            collective_id=0, has_side_effects=True, vmem_limit_bytes=60 * 1024 * 1024
         ),
-    )(tokens, weight_codes, weight_scales, adapter_down, up, rows, adapter_slot, live_rows)
+    )(tokens, weight_codes, weight_scales, down, up, rows, adapter_slot, live_rows)
 
 
 def solution(mesh):

time: 84.4 us -> 70.4 us (0.83)
  the two profiles are of different devices: /device:TPU:8 before, /device:TPU:6 now
where the time goes in v2:
time: 70.4 us; the launch traced here: 69.1 us
  Pallas kernels  67.5 us (96%)
  local copies, waits for them, and re-layouts  1.55 us (2%)
    pallas_call x1, Pallas kernels, body(): pl.pallas_call(kernel, out_shape=jax.ShapeDtypeStruct((group_rows, column...  67.5 us
    unnamed x1, local copies, waits for them, and re-layouts  1.55 us

profile of v2, /device:TPU:6, one launch (start us, length us, event | category | flops | bytes accessed | tf_op | source)
XLA Modules:
  0.0 69.1 jit_solution(9246196307405230897)
XLA Ops:
  0.0 67.5 %shard_map.82 = bf16[32,1664]{1,0:T(8,128)(2,1)} custom-call(bf16[1,16384]{1,0:T(2,128)(2,1)} %tok_hbm.1, bf16[1024,1664]{1,0:T(8,128)(2,1)} %codes_hbm.1, bf16[8,1664]{1,0:T(8,128)(2,1)} %scales_hbm.1, bf16[4,64,512]{2,1,0:T(8,128)(2,1)} %bitcast.4, bf16[256,1664]{1,0:T(8,128)(2,1)} %bitcast.3, s32[4,128]{1,0:T(4,128)} %bitcast.5, s32[64]{0:T(128)} %slot_hbm.1, ...), custom_call_target="tpu_custom_call" | custom-call | tf_op jit(solution)/shard_map/pallas_call | solution.py:574
  67.5 1.5 %copy.10 = bf16[32,1664]{1,0:T(8,128)(2,1)} copy(bf16[32,1664]{1,0:T(8,128)(2,1)} %shard_map.82) | data formatting | bytes 212992

commit v3 on v2

--- a/solution.py
+++ b/solution.py
@@ -136,6 +136,12 @@
         for i in order:
             fn(i)
 
+    def arrived(ref, sem):
+        rcopy(ref, ref, sem, sem, sib).wait_recv()
+
+    def left(ref, sem):
+        rcopy(ref, ref, sem, sem, sib).wait_send()
+
     def each(lo, hi, fn):
         def step(i, carry):
             fn(i)
@@ -167,7 +173,7 @@
             ]
         )
     ]
-    for i in (5, 6, 1, 0, 2, 3, 4, 7):
+    for i in (5, 6, 1, 0):
         loads[i].start()
 
     loads[0].wait()
@@ -214,12 +220,14 @@
             send_down[b, lines, :] = block
 
     each(0, HOMES, choose)
+    for i in (2, 3, 4, 7):
+        loads[i].start()
 
     pl.semaphore_wait(barrier, 2 * (HOMES - 1) + 1)
 
     def down_copy(i):
         b = plane(i)
-        return rcopy(send_down.at[b], got_down.at[g], dwn_s.at[i], dwn_r.at[i], (b, t))
+        return rcopy(send_down.at[b], got_down.at[g], dwn_s.at[0], dwn_r.at[0], (b, t))
 
     swap = rcopy(mine, other, sib_s.at[0], sib_r.at[0], sib)
     swap.start()
@@ -237,11 +245,11 @@
 
     def block_copy(i):
         b = plane(i)
-        return rcopy(pairs.at[b], tiles.at[c, z, g % HALF], blk_s.at[i], blk_r.at[i], (b, t))
+        return rcopy(pairs.at[b], tiles.at[c, z, g % HALF], blk_s.at[0], blk_r.at[0], (b, t))
 
     def slice_copy(i):
         d = layer(i)
-        return rcopy(pairs.at[d], feats.at[z], slc_s.at[i], slc_r.at[i], (g, d * 2 + c))
+        return rcopy(pairs.at[d], feats.at[z], slc_s.at[0], slc_r.at[0], (g, d * 2 + c))
 
     @pl.when(carrier)
     def _():
@@ -281,18 +289,20 @@
 
     each(0, chunks // 2, dequantize)
 
-    def wait_block(i):
-        @pl.when(plane_from(i) // HALF == c)
-        def _():
-            block_copy(i).wait_recv()
-
-    each(1, HOMES, wait_block)
+    @pl.when(carrier)
+    def _():
+        arrived(tiles.at[c, z, pl.ds(0, HALF - 1)], blk_r.at[0])
+
+    @pl.when(jnp.logical_not(carrier))
+    def _():
+        arrived(tiles.at[c, z], blk_r.at[0])
+
 
     far = (6, -6, 3, -3)
 
     def far_copy(n):
         return rcopy(
-            tiles.at[c, z], tiles.at[c, z], zg1_s.at[n], zg1_r.at[n], (g, layer(far[n]) * 2 + c)
+            tiles.at[c, z], tiles.at[c, z], zg1_s.at[0], zg1_r.at[n], (g, layer(far[n]) * 2 + c)
         )
 
     near = [(src, step) for src in (0, -6, 6, -3, 3) for step in (1, -1)]
@@ -300,7 +310,7 @@
     def near_copy(n):
         src, step = near[n]
         s = layer(src)
-        return rcopy(tiles.at[c, s], tiles.at[c, s], zg2_s.at[n], zg2_r.at[n], (g, layer(step) * 2 + c))
+        return rcopy(tiles.at[c, s], tiles.at[c, s], zg2_s.at[0], zg2_r.at[n // 2], (g, layer(step) * 2 + c))
 
     quarter = HALF // 2
 
@@ -308,13 +318,13 @@
         src, step = ((-6, 2), (6, -2))[n]
         s = layer(src)
         some = tiles.at[c, s, pl.ds(n * quarter, quarter)]
-        return rcopy(some, some, zg3_s.at[n], zg3_r.at[n], (g, layer(step) * 2 + c))
+        return rcopy(some, some, zg3_s.at[0], zg3_r.at[0], (g, layer(step) * 2 + c))
 
     begun = [0] + [-d for d in far] + [src - step for src, step in near] + [8]
 
     def pass_copy(n):
         some = tiles.at[c, layer(begun[n])]
-        return rcopy(some, some, pas_s.at[n], pas_r.at[n], sib)
+        return rcopy(some, some, pas_s.at[0], pas_r.at[0], sib)
 
     for n in range(4):
         far_copy(n).start()
@@ -325,14 +335,14 @@
     each(chunks // 2, chunks, dequantize)
     each(0, HOMES, own_mask)
 
-    each(1, LAYERS, lambda i: slice_copy(i).wait_recv())
+    arrived(feats.at[pl.ds(0, LAYERS - 1)], slc_r.at[0])
     shuffle[...] = feats[...].astype(F32).reshape(LAYERS * 16, LANES)
     for j in range(lane_width // LANES):
         low_lhs[:, j * LANES : (j + 1) * LANES] = shuffle[
             pl.ds(c * (lane_width // LANES) + j, group_rows, stride=8), :
         ].astype(BF16)
 
-    each(1, HOMES, lambda i: down_copy(i).wait_recv())
+    arrived(got_down.at[pl.ds(0, HOMES - 1)], dwn_r.at[0])
     chosen = select[...] * lax.dot_general(
         low_lhs[...],
         got_down[...].reshape(HOMES * rank, lane_width),
@@ -348,7 +358,7 @@
     low_send[...] = low.astype(BF16)
 
     def low_copy(i):
-        return rcopy(low_send, low_got.at[z], low_s.at[i], low_r.at[i], (g, layer(i) * 2 + c))
+        return rcopy(low_send, low_got.at[z], low_s.at[0], low_r.at[0], (g, layer(i) * 2 + c))
 
     in_order(along, lambda i: low_copy(i).start())
 
@@ -361,7 +371,7 @@
         pass_copy(1 + n).start()
 
     low_got[z] = jnp.zeros((LAYERS, LANES), BF16)
-    each(1, LAYERS, lambda i: low_copy(i).wait_recv())
+    arrived(low_got.at[pl.ds(0, LAYERS - 1)], low_r.at[0])
     acc = low_sum[...]
     for b in range(LAYERS):
         acc += low_got[b].astype(F32)
@@ -372,20 +382,18 @@
     red_send[...] = (low_sum[...] + low_sib[...]).astype(BF16)
 
     def red_copy(i):
-        return rcopy(red_send, red.at[g], red_s.at[i], red_r.at[i], (plane(i), t))
+        return rcopy(red_send, red.at[g], red_s.at[0], red_r.at[0], (plane(i), t))
 
     in_order(across, lambda i: red_copy(i).start())
     red[g] = red_send[...]
 
-    for n in range(len(near)):
-        near_copy(n).wait_recv()
+    for n in range(0, len(near), 2):
+        arrived(tiles.at[c, pl.ds(0, 2)], zg2_r.at[n // 2])
         pass_copy(5 + n).start()
-    last_copy(0).wait_recv()
-    last_copy(1).wait_recv()
+        pass_copy(6 + n).start()
+    arrived(tiles.at[c, 0], zg3_r.at[0])
     pass_copy(15).start()
-
-    for n in range(LAYERS):
-        pass_copy(n).wait_recv()
+    arrived(tiles.at[1 - c], pas_r.at[0])
 
     def arrange(b):
         shuffle[...] = tiles[b // HALF, :, b % HALF].astype(F32).reshape(LAYERS * 16, LANES)
@@ -395,16 +403,16 @@
 
     each(0, HOMES, arrange)
 
-    def base(k, width):
-        block = dot(lhs[...], weight[:, pl.ds(pl.multiple_of(k * LANES, LANES), width)])
-        for i in range(width // LANES):
-            total[k + i] = block[:, i * LANES : (i + 1) * LANES]
-
-    each(0, chunks // 2, lambda n: base(2 * n, 2 * LANES))
-    if chunks % 2:
-        base(chunks - 1, LANES)
-
-    each(1, HOMES, lambda i: red_copy(i).wait_recv())
+    pair = 2 * LANES
+    spans = [(k, min(pair, columns - k * LANES)) for k in range(0, chunks, 2)]
+
+    def base(j, k, width):
+        total[j, :, :width] = dot(lhs[...], weight[:, k * LANES : k * LANES + width])
+
+    for j, (k, width) in enumerate(spans):
+        base(j, k, width)
+
+    arrived(red.at[pl.ds(0, HOMES - 1)], red_r.at[0])
     spread_from = iota((LANES, 2 * per_home * rank), 0)
     spread_to = iota((LANES, 2 * per_home * rank), 1)
     copies = ones_where(
@@ -433,86 +441,70 @@
         to = lax.rem(second_at + d, SIDE)
         return to, (jnp.where(c == 0, x * SIDE + to, to * SIDE + y), t)
 
-    def part_copy(k, d):
+    def part_copy(j, d):
         to, dev = along_first(d)
-        src = part.at[k, pl.ds(pl.multiple_of(to * four, four), four)]
-        return rcopy(src, got_part.at[k, d - 1], rs1_s.at[k, d - 1], rs1_r.at[k, d - 1], dev)
-
-    def half_copy(k, d):
+        lanes = pl.ds(0, spans[j][1])
+        src = part.at[j, pl.ds(pl.multiple_of(to * four, four), four), lanes]
+        return rcopy(src, got_part.at[j, d - 1, :, lanes], rs1_s.at[0], rs1_r.at[j], dev)
+
+    def half_copy(j, d):
         to, dev = along_second(d)
-        src = half_sum.at[k, pl.ds(pl.multiple_of(to * group_rows, group_rows), group_rows)]
-        return rcopy(src, got_half.at[k, d - 1], rs2_s.at[k, d - 1], rs2_r.at[k, d - 1], dev)
-
-    def send_part(k, width):
-        block = dot(spread[...], up[:, pl.ds(pl.multiple_of(k * LANES, LANES), width)])
-        for i in range(width // LANES):
-            part[k + i] = (total[k + i] + adapter_scale * block[:, i * LANES : (i + 1) * LANES]).astype(BF16)
-            for d in range(1, SIDE):
-                part_copy(k + i, d).start()
-
-    def send_half(k):
-        own = part[k, pl.ds(pl.multiple_of(first_at * four, four), four), :].astype(F32)
+        lanes = pl.ds(0, spans[j][1])
+        src = half_sum.at[j, pl.ds(pl.multiple_of(to * group_rows, group_rows), group_rows), lanes]
+        return rcopy(src, got_half.at[j, d - 1, :, lanes], rs2_s.at[0], rs2_r.at[j], dev)
+
+    def send_part(j):
+        k, width = spans[j]
+        block = adapter_scale * dot(spread[...], up[:, k * LANES : k * LANES + width])
+        part[j, :, :width] = (total[j, :, :width] + block).astype(BF16)
         for d in range(1, SIDE):
-            part_copy(k, d).wait_recv()
-            own += got_part[k, d - 1].astype(F32)
-        half_sum[k] = own.astype(BF16)
+            part_copy(j, d).start()
+
+    def send_half(j):
+        k, width = spans[j]
+        arrived(got_part.at[j, :, :, pl.ds(0, width)], rs1_r.at[j])
+        own = part[j, pl.ds(pl.multiple_of(first_at * four, four), four), :width].astype(F32)
         for d in range(1, SIDE):
-            half_copy(k, d).start()
-
-    lead = 4
-
-    def both(n):
-        send_part(2 * n + lead, 2 * LANES)
-        send_half(2 * n)
-        send_half(2 * n + 1)
-
-    each(0, lead // 2, lambda n: send_part(2 * n, 2 * LANES))
-    each(0, (chunks - lead) // 2, both)
-    if chunks % 2:
-        send_part(chunks - 1, LANES)
-    each((chunks - lead) // 2 * 2, chunks, send_half)
+            own += got_part[j, d - 1, :, :width].astype(F32)
+        half_sum[j, :, :width] = own.astype(BF16)
+        for d in range(1, SIDE):
+            half_copy(j, d).start()
+
+    lead = 2
+    for j in range(len(spans) + lead):
+        if j < len(spans):
+            send_part(j)
+        if j >= lead:
+            send_half(j - lead)
 
     loads[7].wait()
-    live = iota((group_rows, LANES), 0) < live_ref[g]
-
-    def finish(k):
-        own = half_sum[k, pl.ds(pl.multiple_of(second_at * group_rows, group_rows), group_rows), :].astype(F32)
+    live = iota((group_rows, pair), 0) < live_ref[g]
+
+    for j, (k, width) in enumerate(spans):
+        arrived(got_half.at[j, :, :, pl.ds(0, width)], rs2_r.at[j])
+        own = half_sum[j, pl.ds(pl.multiple_of(second_at * group_rows, group_rows), group_rows), :width].astype(F32)
         for d in range(1, SIDE):
-            half_copy(k, d).wait_recv()
-            own += got_half[k, d - 1].astype(F32)
-        out_ref[:, pl.ds(pl.multiple_of(k * LANES, LANES), LANES)] = jnp.where(live, own, 0.0).astype(BF16)
-
-    each(0, chunks, finish)
+            own += got_half[j, d - 1, :, :width].astype(F32)
+        out_ref[:, k * LANES : k * LANES + width] = jnp.where(live[:, :width], own, 0.0).astype(BF16)
 
     swap.wait_send()
     swap_low.wait_send()
 
     @pl.when(carrier)
     def _():
-        each(1, HOMES, lambda i: block_copy(i).wait_send())
-
-    def sent(i):
-        slice_copy(i).wait_send()
-        down_copy(i).wait_send()
-        low_copy(i).wait_send()
-        red_copy(i).wait_send()
-
-    each(1, HOMES, sent)
-    for n in range(4):
-        far_copy(n).wait_send()
-    for n in range(len(near)):
-        near_copy(n).wait_send()
-    last_copy(0).wait_send()
-    last_copy(1).wait_send()
-    for n in range(LAYERS):
-        pass_copy(n).wait_send()
-
-    def sent_parts(k):
-        for d in range(1, SIDE):
-            part_copy(k, d).wait_send()
-            half_copy(k, d).wait_send()
-
-    each(0, chunks, sent_parts)
+        left(feats.at[pl.ds(0, HOMES - 1)], blk_s.at[0])
+
+    left(feats.at[pl.ds(0, LAYERS - 1)], slc_s.at[0])
+    left(got_down.at[pl.ds(0, HOMES - 1)], dwn_s.at[0])
+    left(low_got.at[pl.ds(0, LAYERS - 1)], low_s.at[0])
+    left(red.at[pl.ds(0, HOMES - 1)], red_s.at[0])
+    left(tiles.at[c, pl.ds(0, len(far))], zg1_s.at[0])
+    left(tiles.at[c, pl.ds(0, len(near))], zg2_s.at[0])
+    left(tiles.at[c, 0], zg3_s.at[0])
+    left(tiles.at[c], pas_s.at[0])
+    for j, (k, width) in enumerate(spans):
+        left(got_part.at[j, :, :, pl.ds(0, width)], rs1_s.at[0])
+        left(got_half.at[j, :, :, pl.ds(0, width)], rs2_s.at[0])
 
 
 def body(tokens, weight_codes, weight_scales, adapter_down, adapter_up, row_adapter, adapter_slot, live_rows):
@@ -524,6 +516,7 @@
     group_rows = all_rows // HOMES
     chunks = columns // LANES
     wide = per_home * rank
+    pairs = (chunks + 1) // 2
     up = adapter_up.reshape(wide, columns)
     rows = row_adapter.reshape(all_rows // LANES, LANES)
     vmem, dma = pltpu.VMEM, pltpu.SemaphoreType.DMA
@@ -559,18 +552,17 @@
         vmem((HOMES * LAYERS, 2 * wide), F32),
         vmem((all_rows, wide), BF16),
         vmem((all_rows, wide), F32),
-        vmem((chunks, all_rows, LANES), F32),
-        vmem((chunks, all_rows, LANES), BF16),
-        vmem((chunks, SIDE - 1, SIDE * group_rows, LANES), BF16),
-        vmem((chunks, SIDE * group_rows, LANES), BF16),
-        vmem((chunks, SIDE - 1, group_rows, LANES), BF16),
+        vmem((pairs, all_rows, 2 * LANES), F32),
+        vmem((pairs, all_rows, 2 * LANES), BF16),
+        vmem((pairs, SIDE - 1, SIDE * group_rows, 2 * LANES), BF16),
+        vmem((pairs, SIDE * group_rows, 2 * LANES), BF16),
+        vmem((pairs, SIDE - 1, group_rows, 2 * LANES), BF16),
         dma((8,)),
-        dma((3,)),
-        dma((3,)),
+        dma((2,)),
+        dma((2,)),
     ]
-    for count in (HOMES, LAYERS, HOMES, 4, 10, 2, LAYERS, LAYERS, HOMES):
-        scratch += [dma((count,)), dma((count,))]
-    scratch += [dma((chunks, SIDE - 1))] * 4
+    for count in (1, 1, 1, 4, 5, 1, 1, 1, 1, pairs, pairs):
+        scratch += [dma((1,)), dma((count,))]
     return pl.pallas_call(
         kernel,
         out_shape=jax.ShapeDtypeStruct((group_rows, columns), BF16),

time: 70.4 us -> 66.3 us (0.942)
  Pallas kernels: 67.5 us -> 63.5 us
    pallas_call x1, Pallas kernels: 67.5 us -> 63.5 us  [body(): pl.pallas_call(kernel, out_shape=jax.ShapeDtypeStruct((group_rows, column...]
where the time goes in v3:
time: 66.3 us; the launch traced here: 65.1 us
  Pallas kernels  63.5 us (96%)
  local copies, waits for them, and re-layouts  1.55 us (2%)
    pallas_call x1, Pallas kernels, body(): pl.pallas_call(kernel, out_shape=jax.ShapeDtypeStruct((group_rows, column...  63.5 us
    unnamed x1, local copies, waits for them, and re-layouts  1.55 us

profile of v3, /device:TPU:6, one launch (start us, length us, event | category | flops | bytes accessed | tf_op | source)
XLA Modules:
  0.0 65.1 jit_solution(16390685749213774268)
XLA Ops:
  0.0 63.5 %shard_map.82 = bf16[32,1664]{1,0:T(8,128)(2,1)} custom-call(bf16[1,16384]{1,0:T(2,128)(2,1)} %tok_hbm.1, bf16[1024,1664]{1,0:T(8,128)(2,1)} %codes_hbm.1, bf16[8,1664]{1,0:T(8,128)(2,1)} %scales_hbm.1, bf16[4,64,512]{2,1,0:T(8,128)(2,1)} %bitcast.4, bf16[256,1664]{1,0:T(8,128)(2,1)} %bitcast.3, s32[4,128]{1,0:T(4,128)} %bitcast.5, s32[64]{0:T(128)} %slot_hbm.1, ...), custom_call_target="tpu_custom_call" | custom-call | tf_op jit(solution)/shard_map/pallas_call | solution.py:566
  63.6 1.5 %copy.10 = bf16[32,1664]{1,0:T(8,128)(2,1)} copy(bf16[32,1664]{1,0:T(8,128)(2,1)} %shard_map.82) | data formatting | bytes 212992

commit v4 on v3

--- a/solution.py
+++ b/solution.py
@@ -412,13 +412,13 @@
     for j, (k, width) in enumerate(spans):
         base(j, k, width)
 
-    arrived(red.at[pl.ds(0, HOMES - 1)], red_r.at[0])
     spread_from = iota((LANES, 2 * per_home * rank), 0)
     spread_to = iota((LANES, 2 * per_home * rank), 1)
     copies = ones_where(
         spread_from == spread_to % rank + (spread_to // (per_home * rank)) * rank
     )
     wide = per_home * rank
+    arrived(red.at[pl.ds(0, HOMES - 1)], red_r.at[0])
     expand[...] = dot(red[...].reshape(HOMES * LAYERS, LANES), copies)
     for b in range(HOMES):
         here = pl.multiple_of(place(b) * group_rows, group_rows)
@@ -457,7 +457,7 @@
         k, width = spans[j]
         block = adapter_scale * dot(spread[...], up[:, k * LANES : k * LANES + width])
         part[j, :, :width] = (total[j, :, :width] + block).astype(BF16)
-        for d in range(1, SIDE):
+        for d in (2, 1, 3):
             part_copy(j, d).start()
 
     def send_half(j):
@@ -467,10 +467,10 @@
         for d in range(1, SIDE):
             own += got_part[j, d - 1, :, :width].astype(F32)
         half_sum[j, :, :width] = own.astype(BF16)
-        for d in range(1, SIDE):
+        for d in (2, 1, 3):
             half_copy(j, d).start()
 
-    lead = 2
+    lead = 3
     for j in range(len(spans) + lead):
         if j < len(spans):
             send_part(j)

time: 66.3 us -> 65 us (0.980)
  Pallas kernels: 63.5 us -> 62.7 us
    pallas_call x1, Pallas kernels: 63.5 us -> 62.7 us  [body(): pl.pallas_call(kernel, out_shape=jax.ShapeDtypeStruct((group_rows, column...]
where the time goes in v4:
time: 65 us; the launch traced here: 64.2 us
  Pallas kernels  62.7 us (96%)
  local copies, waits for them, and re-layouts  1.55 us (2%)
    pallas_call x1, Pallas kernels, body(): pl.pallas_call(kernel, out_shape=jax.ShapeDtypeStruct((group_rows, column...  62.7 us
    unnamed x1, local copies, waits for them, and re-layouts  1.55 us

profile of v4, /device:TPU:6, one launch (start us, length us, event | category | flops | bytes accessed | tf_op | source)
XLA Modules:
  0.0 64.2 jit_solution(929282730604425350)
XLA Ops:
  0.0 62.7 %shard_map.82 = bf16[32,1664]{1,0:T(8,128)(2,1)} custom-call(bf16[1,16384]{1,0:T(2,128)(2,1)} %tok_hbm.1, bf16[1024,1664]{1,0:T(8,128)(2,1)} %codes_hbm.1, bf16[8,1664]{1,0:T(8,128)(2,1)} %scales_hbm.1, bf16[4,64,512]{2,1,0:T(8,128)(2,1)} %bitcast.4, bf16[256,1664]{1,0:T(8,128)(2,1)} %bitcast.3, s32[4,128]{1,0:T(4,128)} %bitcast.5, s32[64]{0:T(128)} %slot_hbm.1, ...), custom_call_target="tpu_custom_call" | custom-call | tf_op jit(solution)/shard_map/pallas_call | solution.py:566
  62.7 1.5 %copy.10 = bf16[32,1664]{1,0:T(8,128)(2,1)} copy(bf16[32,1664]{1,0:T(8,128)(2,1)} %shard_map.82) | data formatting | bytes 212992
